TPU v7x, 32 devices: a whole 2x2x4 slice. The times are simulated.
32 devices in a mesh: groups: 2 (over x), band: 16 (over z, y, core).
Axes of the slice: x: 2, y: 2, z: 4, core: 2. Of those that a mesh axis runs over, the one named last changes fastest.
Arguments:
- factor: bfloat16 [32768, 128], P(('groups', 'band')), parts along dimension 0
- near_vals: bfloat16 [512, 5, 64, 64], P(('groups', 'band')), parts along dimension 0, may hold values from 0.049804688 to 4
- far_vals: bfloat16 [32768, 512], P(('groups', 'band')), parts along dimension 0, may hold values from 0.049804688 to 4
- pub_rows: int32 [32, 32], P(('groups', 'band')), parts along dimension 0, may hold values from 0 to 1023
- far_count: int32 [32, 16], P(('groups', 'band')), parts along dimension 0, may hold values from 1 to 32, as said below
Outputs:
- updated: float32 [32768, 128], P(('groups', 'band')), parts along dimension 0
There are 2 independent parts, one for each index of `groups`. A program takes and returns all parts, laid end to end along the dimension named above; each array names one. Nothing has to cross between parts.
Inputs may be any that keep to these rules, and one draw needn't show every extreme that they name: `far_count`: in every row some entry equals 32.
All inputs are finite; a program needn't handle non-finite values.
Results may differ from a plain program's by a relative error of at most 0.0003.
Values may be sent and summed in bfloat16 or wider, within the bound.
A program may use at most 64 MiB of HBM per device.

v0:
```python
import jax
import jax.numpy as jnp
from jax import lax
from jax.sharding import PartitionSpec as P

BLOCK = 64
HALF_BLOCKS = 2


def extended(shard, sides, width):
    for axis, dim in sides:
        peers, length = (lax.axis_size(axis), shard.shape[dim])
        up = [(i, (i + 1) % peers) for i in range(peers - 1)]
        down = [(j, i) for i, j in up]
        last = lax.slice_in_dim(shard, length - width, length, axis=dim)
        first = lax.slice_in_dim(shard, 0, width, axis=dim)
        before = lax.ppermute(last, axis, up)
        after = lax.ppermute(first, axis, down)
        shard = jnp.concatenate([before, shard, after], axis=dim)
    return shard


def shards(factor, near_vals, far_vals, pub_rows, far_count):
    row_count, rank_width = factor.shape
    band_size = lax.axis_size("band")
    margin = HALF_BLOCKS * BLOCK
    padded = extended(factor, (("band", 0),), margin)
    block_count = row_count // BLOCK
    blocks = padded.reshape(block_count + 2 * HALF_BLOCKS, BLOCK, rank_width)
    near_sum = jnp.zeros((block_count, BLOCK, rank_width), jnp.float32)
    for offset in range(2 * HALF_BLOCKS + 1):
        near_sum = near_sum + jnp.einsum(
            "bij,bjk->bik",
            near_vals[:, offset],
            blocks[offset : offset + block_count],
            preferred_element_type=jnp.float32,
        )
    near_sum = near_sum.reshape(row_count, rank_width)
    slot_count = pub_rows.shape[1]
    chosen = jnp.take(factor, pub_rows[0], axis=0)
    slot_index = jnp.arange(band_size * slot_count, dtype=jnp.int32) % slot_count
    live_slots = slot_index < jnp.repeat(far_count[0], slot_count)
    masked = jnp.where(live_slots[None, :], far_vals, jnp.zeros((), far_vals.dtype))
    own_gram = lax.dot_general(
        factor, factor, (((0,), (0,)), ((), ())), preferred_element_type=jnp.float32
    )
    gram_matrix = lax.psum(own_gram, "band")
    arrived = lax.all_gather(chosen, "band", axis=0, tiled=True)
    far_sum = jnp.dot(masked, arrived, preferred_element_type=jnp.float32)
    lower_factor = jnp.linalg.cholesky(gram_matrix)
    inverse = jax.scipy.linalg.cho_solve(
        (lower_factor, True), jnp.eye(rank_width, dtype=jnp.float32)
    )
    return jnp.dot(near_sum + far_sum, inverse, precision=lax.Precision.HIGHEST)


def solution(mesh):
    placed = (
        P(("groups", "band"), None),
        P(("groups", "band"), None, None, None),
        P(("groups", "band"), None),
        P(("groups", "band"), None),
        P(("groups", "band"), None),
    )
    return jax.shard_map(
        shards, mesh=mesh, in_specs=placed, out_specs=P(("groups", "band"), None), check_vma=False
    )
```

profile of v0, /device:TPU:8, one launch (start us, length us, event | category | flops | bytes accessed | tf_op | source)
XLA Modules:
  0.0 138.6 jit_solution(12282025486069231995)
XLA Ops:
  6.5 0.8 fusion.33
  7.4 1.9 %collective-permute-start = (bf16[128,128]{1,0:T(8,128)(2,1)S(1)}, bf16[128,128]{1,0:T(8,128)(2,1)S(1)}, u32[]{:S(2)}, u32[]{:S(2)}) collective-permute-start(bf16[128,128]{1,0:T(8,128)(2,1)S(1)} %get-tuple-element.11), channel_id=1, source_target_pairs={{0,1},{1,2},{2,3},{3,4},{4,5},{5,6},{6,7},{7,8},{8,9},{9,10},{10,1... | collective-permute-start | bytes 98312 | tf_op jit(solution)/shard_map/ppermute | solution.py:17
  9.3 4.5 %collective-permute-start.1 = (bf16[128,128]{1,0:T(8,128)(2,1)S(1)}, bf16[128,128]{1,0:T(8,128)(2,1)S(1)}, u32[]{:S(2)}, u32[]{:S(2)}) collective-permute-start(bf16[128,128]{1,0:T(8,128)(2,1)S(1)} %get-tuple-element.12), channel_id=1, source_target_pairs={{1,0},{2,1},{3,2},{4,3},{5,4},{6,5},{7,6},{8,7},{9,8},{10,9},{11,1... | collective-permute-start | bytes 98312 | tf_op jit(solution)/shard_map/ppermute | solution.py:18
  13.8 1.9 %fusion.34 = f32[128,128]{0,1:T(8,128)} fusion(bf16[1024,128]{1,0:T(8,128)(2,1)} %param.5), kind=kOutput, calls=%fused_computation.56 | convolution fusion | flops 33554432 | bytes 327680 | tf_op jit(solution)/shard_map/dot_general | solution.py:44
  15.8 0.0 all-reduce.2.cloned.1.call-update
  15.8 0.7 fusion.29
  16.5 0.7 compare_and_fusion
  17.1 1.6 %gather_fusion = bf16[32,128]{1,0:T(8,128)(2,1)S(1)} fusion(bf16[1024,128]{1,0:T(8,128)(2,1)} %param.5, s32[1024]{0:T(1024)S(1)} %pad_clamp_fusion), kind=kCustom, calls=%fused_computation | custom fusion | bytes 16512 | tf_op jit(solution)/shard_map/jit(_take)/gather | solution.py:40
  18.7 0.7 broadcast_in_dim.28
  19.4 0.1 reshape.74
  19.5 1.3 fusion.9
  20.9 0.1 broadcast_select_fusion
  20.9 19.7 %all_gather.3 = bf16[512,128]{1,0:T(8,128)(2,1)} all-gather(bf16[32,128]{1,0:T(8,128)(2,1)S(1)} %broadcast_select_fusion), channel_id=1, replica_groups=mesh['groups'=2,'band'=16] {'band'}, dimensions={0}, use_global_device_ids=true | all-gather | bytes 139264 | tf_op jit(solution)/shard_map/all_gather | solution.py:48
  40.6 0.1 constant_dynamic-update-slice_fusion
  40.7 0.2 fusion.11
  41.0 0.2 convolution_bitcast_fusion
  41.2 62.1 %all-reduce.2.cloned.1.call-done = f32[128,128]{0,1:T(8,128)} async-done(((f32[128,128]{0,1:T(8,128)}), f32[128,128]{0,1:T(8,128)}) %all-reduce.2.cloned.1.call-update) | async-done | bytes 65552 | tf_op jit(solution)/shard_map/psum | solution.py:47
  103.3 0.9 copy.12
  104.2 0.9 fusion.24
  105.1 11.7 %cholesky.17 = f32[128,128]{1,0:T(8,128)S(1)} custom-call(f32[128,128]{1,0:T(8,128)S(1)} %fusion.24), custom_call_target="Cholesky" | custom-call | tf_op jit(solution)/shard_map/jit(cholesky)/cholesky | solution.py:50
  116.8 0.6 compare_reduce_fusion
  117.5 0.7 fusion.19
  118.1 9.8 %custom-call.10 = f32[1,128,128]{1,2,0:T(8,128)S(1)} custom-call(f32[1,128,128]{2,1,0:T(8,128)S(1)} %fusion.19), custom_call_target="InvertDiagBlocksLowerTriangular" | custom-call | tf_op jit(solution)/shard_map/jit(_cho_solve)/triangular_solve | solution.py:51
  128.0 0.2 fusion.22
  128.2 0.2 fusion.20
  128.4 0.2 fusion.3
  128.7 0.0 copy-start.3
  128.7 0.2 fusion.1
  128.9 0.7 copy-done.2
  129.6 0.4 copy-done.3
  130.0 0.4 convolution_add_fusion
  130.4 1.4 fusion.35
  (15 shorter events, 0.2 us)
Async XLA Ops:
  6.5 34.1 %copy-start = (bf16[1024,128]{1,0:T(8,128)(2,1)S(1)}, bf16[1024,128]{1,0:T(8,128)(2,1)}, u32[]{:S(2)}) copy-start(bf16[1024,128]{1,0:T(8,128)(2,1)} %param.5) | copy-start | bytes 786436
  6.5 96.8 %all-reduce.2.cloned.1.call-start = ((), (), s32[]{:S(2)}) async-start(), calls=%async_computation | async-start | bytes 131072 | tf_op jit(solution)/shard_map/psum | solution.py:47
  7.4 33.2 %collective-permute-start = (bf16[128,128]{1,0:T(8,128)(2,1)S(1)}, bf16[128,128]{1,0:T(8,128)(2,1)S(1)}, u32[]{:S(2)}, u32[]{:S(2)}) collective-permute-start(bf16[128,128]{1,0:T(8,128)(2,1)S(1)} %get-tuple-element.11), channel_id=1, source_target_pairs={{0,1},{1,2},{2,3},{3,4},{4,5},{5,6},{6,7},{7,8},{8,9},{9,10},{10,1... | collective-permute-start | bytes 98312 | tf_op jit(solution)/shard_map/ppermute | solution.py:17
  9.3 31.7 %collective-permute-start.1 = (bf16[128,128]{1,0:T(8,128)(2,1)S(1)}, bf16[128,128]{1,0:T(8,128)(2,1)S(1)}, u32[]{:S(2)}, u32[]{:S(2)}) collective-permute-start(bf16[128,128]{1,0:T(8,128)(2,1)S(1)} %get-tuple-element.12), channel_id=1, source_target_pairs={{1,0},{2,1},{3,2},{4,3},{5,4},{6,5},{7,6},{8,7},{9,8},{10,9},{11,1... | collective-permute-start | bytes 98312 | tf_op jit(solution)/shard_map/ppermute | solution.py:18
  19.5 21.2 %copy-start.1 = (bf16[16,5,64,64]{3,2,1,0:T(8,128)(2,1)S(1)}, bf16[16,5,64,64]{3,2,1,0:T(8,128)(2,1)}, u32[]{:S(2)}) copy-start(bf16[16,5,64,64]{3,2,1,0:T(8,128)(2,1)} %param.6) | copy-start | bytes 1966084
  128.6 0.9 copy-start.2
  128.7 1.3 copy-start.3
Sparse Core Ops, SparseCore 0:
  15.9 87.3 all-reduce.1
where the time goes:
time: 139 us
  waiting for transfers between devices  62.1 us (45%)
  other arithmetic  25.1 us (18%)
  blocking collectives  19.7 us (14%)
  between operations  13.5 us (10%)
  starting transfers between devices  6.45 us (5%)
  matrix products  6.39 us (5%)
  local copies, waits for them, and re-layouts  5.35 us (4%)
    psum x1, waiting for transfers between devices, shards(): gram_matrix = lax.psum(own_gram, 'band')  62.1 us
    all_gather x1, blocking collectives, shards(): arrived = lax.all_gather(chosen, 'band', axis=0, tiled=True)  19.7 us
    another operation x3, other arithmetic, shards(): lower_factor = jnp.linalg.cholesky(gram_matrix)  12.4 us
    another operation x2, other arithmetic, shards(): jax.scipy.linalg.cho_solve((lower_factor, True), jnp.eye(rank_width, dtyp...  10.5 us
    ppermute x1, starting transfers between devices, extended(): after = lax.ppermute(first, axis, down)  4.54 us
  transfers between devices with their start and end apart: 3, of which 1 were waited for; matrix products, arithmetic and copies ran while one was open for 6% of the time, Pallas kernels for 0%

commit v1 on v0

--- a/solution.py
+++ b/solution.py
@@ -44,7 +44,10 @@
     own_gram = lax.dot_general(
         factor, factor, (((0,), (0,)), ((), ())), preferred_element_type=jnp.float32
     )
-    gram_matrix = lax.psum(own_gram, "band")
+    size, gram_matrix = (lax.axis_size("band"), own_gram)
+    for far in [1 << k for k in range(size.bit_length() - 1)]:
+        route = [(i_2, i_2 ^ far) for i_2 in range(size)]
+        gram_matrix = gram_matrix + lax.ppermute(gram_matrix, "band", route)
     arrived = lax.all_gather(chosen, "band", axis=0, tiled=True)
     far_sum = jnp.dot(masked, arrived, preferred_element_type=jnp.float32)
     lower_factor = jnp.linalg.cholesky(gram_matrix)

time: 139 us -> 76.3 us (0.55)
  the two profiles are of different devices: /device:TPU:8 before, /device:TPU:0 now
where the time goes in v1:
time: 76.3 us; the launch traced here: 76 us
  blocking collectives  25.3 us (33%)
  other arithmetic  24.3 us (32%)
  waiting for transfers between devices  13 us (17%)
  matrix products  5.82 us (8%)
  starting transfers between devices  3.97 us (5%)
  local copies, waits for them, and re-layouts  3.4 us (4%)
    all_gather x1, blocking collectives, shards(): arrived = lax.all_gather(chosen, 'band', axis=0, tiled=True)  25.3 us
    ppermute x4, waiting for transfers between devices, shards(): gram_matrix = gram_matrix + lax.ppermute(gram_matrix, 'band', route)  13 us
    another operation x3, other arithmetic, shards(): lower_factor = jnp.linalg.cholesky(gram_matrix)  12.4 us
    another operation x2, other arithmetic, shards(): jax.scipy.linalg.cho_solve((lower_factor, True), jnp.eye(rank_width, dtyp...  10.5 us
    dot_general x5, matrix products, shards(): jnp.einsum('bij,bjk->bik', near_vals[:, offset], blocks[offset:offset + b...  2.2 us
    ppermute x1, starting transfers between devices, extended(): before = lax.ppermute(last, axis, up)  1.95 us
    gather x1, local copies, waits for them, and re-layouts, shards(): chosen = jnp.take(factor, pub_rows[0], axis=0)  1.57 us
  transfers between devices with their start and end apart: 6, of which 3 were waited for; matrix products, arithmetic and copies ran while one was open for 10% of the time, Pallas kernels for 0%

profile of v1, /device:TPU:0, one launch (start us, length us, event | category | flops | bytes accessed | tf_op | source)
XLA Modules:
  0.0 76.0 jit_solution(3772377194736837126)
XLA Ops:
  0.0 1.4 %fusion.34 = f32[128,128]{0,1:T(8,128)S(1)} fusion(bf16[1024,128]{1,0:T(8,128)(2,1)} %param.5), kind=kOutput, calls=%fused_computation.56 | convolution fusion | flops 33554432 | bytes 327680 | tf_op jit(solution)/shard_map/dot_general | solution.py:44
  1.4 0.5 collective-permute-start.2
  1.9 0.8 %fusion.33 = (bf16[128,128]{1,0:T(8,128)(2,1)S(1)}, bf16[128,128]{1,0:T(8,128)(2,1)S(1)}) fusion(bf16[1024,128]{1,0:T(8,128)(2,1)} %param.5), kind=kLoop, calls=%fused_computation.55 | loop fusion | bytes 131072 | tf_op jit(solution)/shard_map/slice | solution.py:15
  2.7 2.0 %collective-permute-start = (bf16[128,128]{1,0:T(8,128)(2,1)S(1)}, bf16[128,128]{1,0:T(8,128)(2,1)S(1)}, u32[]{:S(2)}, u32[]{:S(2)}) collective-permute-start(bf16[128,128]{1,0:T(8,128)(2,1)S(1)} %get-tuple-element.11), channel_id=1, source_target_pairs={{0,1},{1,2},{2,3},{3,4},{4,5},{5,6},{6,7},{7,8},{8,9},{9,10},{10,1... | collective-permute-start | bytes 98312 | tf_op jit(solution)/shard_map/ppermute | solution.py:17
  4.6 1.3 %collective-permute-start.1 = (bf16[128,128]{1,0:T(8,128)(2,1)S(1)}, bf16[128,128]{1,0:T(8,128)(2,1)S(1)}, u32[]{:S(2)}, u32[]{:S(2)}) collective-permute-start(bf16[128,128]{1,0:T(8,128)(2,1)S(1)} %get-tuple-element.12), channel_id=1, source_target_pairs={{1,0},{2,1},{3,2},{4,3},{5,4},{6,5},{7,6},{8,7},{9,8},{10,9},{11,1... | collective-permute-start | bytes 98312 | tf_op jit(solution)/shard_map/ppermute | solution.py:18
  5.9 0.7 fusion.29
  6.6 0.7 compare_and_fusion
  7.3 1.6 %gather_fusion = bf16[32,128]{1,0:T(8,128)(2,1)S(1)} fusion(bf16[1024,128]{1,0:T(8,128)(2,1)} %param.5, s32[1024]{0:T(1024)S(1)} %pad_clamp_fusion), kind=kCustom, calls=%fused_computation | custom fusion | bytes 16512 | tf_op jit(solution)/shard_map/jit(_take)/gather | solution.py:40
  8.8 0.7 broadcast_in_dim.28
  9.6 0.1 reshape.74
  9.7 1.3 %fusion.9 = f32[16,64,128]{2,1,0:T(8,128)S(1)} fusion(bf16[16,64,128]{2,1,0:T(8,128)(2,1)} %bitcast.72, bf16[16,5,64,64]{3,2,1,0:T(8,128)(2,1)} %param.6), kind=kOutput, calls=%fused_computation.14 | convolution fusion | flops 16777216 | bytes 1048576 | tf_op jit(solution)/shard_map/bij,bjk->bik/dot_general | solution.py:32
  11.0 0.1 broadcast_select_fusion
  11.1 25.3 %all_gather.3 = bf16[512,128]{1,0:T(8,128)(2,1)S(1)} all-gather(bf16[32,128]{1,0:T(8,128)(2,1)S(1)} %broadcast_select_fusion), channel_id=1, replica_groups=mesh['groups'=2,'band'=16] {'band'}, dimensions={0}, use_global_device_ids=true | all-gather | bytes 139264 | tf_op jit(solution)/shard_map/all_gather | solution.py:51
  36.5 0.2 fusion.11
  36.7 0.2 fusion.3
  37.0 0.1 collective-permute-start.3
  37.1 0.2 convolution_bitcast_fusion
  37.3 4.1 %collective-permute-done.3 = f32[128,128]{0,1:T(8,128)S(1)} collective-permute-done((f32[128,128]{0,1:T(8,128)S(1)}, f32[128,128]{0,1:T(8,128)S(1)}, u32[]{:S(2)}, u32[]{:S(2)}) %collective-permute-start.3) | collective-permute-done | bytes 65568 | tf_op jit(solution)/shard_map/ppermute | solution.py:50
  41.5 0.1 collective-permute-start.4
  41.5 0.2 fusion.1
  41.7 4.0 %collective-permute-done.4 = f32[128,128]{0,1:T(8,128)S(1)} collective-permute-done((f32[128,128]{0,1:T(8,128)S(1)}, f32[128,128]{0,1:T(8,128)S(1)}, u32[]{:S(2)}, u32[]{:S(2)}) %collective-permute-start.4) | collective-permute-done | bytes 65568 | tf_op jit(solution)/shard_map/ppermute | solution.py:50
  45.8 0.1 collective-permute-start.5
  45.9 0.4 convolution_add_fusion
  46.3 4.8 %collective-permute-done.5 = f32[128,128]{0,1:T(8,128)S(1)} collective-permute-done((f32[128,128]{0,1:T(8,128)S(1)}, f32[128,128]{0,1:T(8,128)S(1)}, u32[]{:S(2)}, u32[]{:S(2)}) %collective-permute-start.5) | collective-permute-done | bytes 65568 | tf_op jit(solution)/shard_map/ppermute | solution.py:50
  51.2 0.1 copy.13
  51.3 11.7 %cholesky.17 = f32[128,128]{1,0:T(8,128)S(1)} custom-call(f32[128,128]{1,0:T(8,128)S(1)} %fusion.24), custom_call_target="Cholesky" | custom-call | tf_op jit(solution)/shard_map/jit(cholesky)/cholesky | solution.py:53
  63.0 0.6 compare_reduce_fusion
  63.7 0.7 fusion.19
  64.4 9.8 %custom-call.10 = f32[1,128,128]{1,2,0:T(8,128)S(1)} custom-call(f32[1,128,128]{2,1,0:T(8,128)S(1)} %fusion.19), custom_call_target="InvertDiagBlocksLowerTriangular" | custom-call | tf_op jit(solution)/shard_map/jit(_cho_solve)/triangular_solve | solution.py:54
  74.2 0.2 fusion.22
  74.4 0.2 fusion.20
  74.6 1.4 %fusion.35 = f32[1024,128]{1,0:T(8,128)} fusion(f32[1024,128]{1,0:T(8,128)S(1)} %convolution_add_fusion, f32[128,128]{1,0:T(8,128)S(1)} %fusion.20), kind=kOutput, calls=%fused_computation.57 | convolution fusion | flops 201326592 | bytes 1114112 | tf_op jit(solution)/shard_map/dot_general | solution.py:57
  (22 shorter events, 0.3 us)
Async XLA Ops:
  0.0 36.4 %copy-start = (bf16[1024,128]{1,0:T(8,128)(2,1)S(1)}, bf16[1024,128]{1,0:T(8,128)(2,1)}, u32[]{:S(2)}) copy-start(bf16[1024,128]{1,0:T(8,128)(2,1)} %param.5) | copy-start | bytes 786436
  1.4 35.6 %collective-permute-start.2 = (f32[128,128]{0,1:T(8,128)S(1)}, f32[128,128]{0,1:T(8,128)S(1)}, u32[]{:S(2)}, u32[]{:S(2)}) collective-permute-start(f32[128,128]{0,1:T(8,128)S(1)} %fusion.34), channel_id=1, source_target_pairs={{0,1},{1,0},{2,3},{3,2},{4,5},{5,4},{6,7},{7,6},{8,9},{9,8},{10,11... | collective-permute-start | bytes 196616 | tf_op jit(solution)/shard_map/ppermute | solution.py:50
  2.7 33.7 %collective-permute-start = (bf16[128,128]{1,0:T(8,128)(2,1)S(1)}, bf16[128,128]{1,0:T(8,128)(2,1)S(1)}, u32[]{:S(2)}, u32[]{:S(2)}) collective-permute-start(bf16[128,128]{1,0:T(8,128)(2,1)S(1)} %get-tuple-element.11), channel_id=1, source_target_pairs={{0,1},{1,2},{2,3},{3,4},{4,5},{5,6},{6,7},{7,8},{8,9},{9,10},{10,1... | collective-permute-start | bytes 98312 | tf_op jit(solution)/shard_map/ppermute | solution.py:17
  4.6 32.3 %collective-permute-start.1 = (bf16[128,128]{1,0:T(8,128)(2,1)S(1)}, bf16[128,128]{1,0:T(8,128)(2,1)S(1)}, u32[]{:S(2)}, u32[]{:S(2)}) collective-permute-start(bf16[128,128]{1,0:T(8,128)(2,1)S(1)} %get-tuple-element.12), channel_id=1, source_target_pairs={{1,0},{2,1},{3,2},{4,3},{5,4},{6,5},{7,6},{8,7},{9,8},{10,9},{11,1... | collective-permute-start | bytes 98312 | tf_op jit(solution)/shard_map/ppermute | solution.py:18
  9.7 26.8 %copy-start.1 = (bf16[16,5,64,64]{3,2,1,0:T(8,128)(2,1)S(1)}, bf16[16,5,64,64]{3,2,1,0:T(8,128)(2,1)}, u32[]{:S(2)}) copy-start(bf16[16,5,64,64]{3,2,1,0:T(8,128)(2,1)} %param.6) | copy-start | bytes 1966084
  37.0 4.4 %collective-permute-start.3 = (f32[128,128]{0,1:T(8,128)S(1)}, f32[128,128]{0,1:T(8,128)S(1)}, u32[]{:S(2)}, u32[]{:S(2)}) collective-permute-start(f32[128,128]{0,1:T(8,128)S(1)} %add.87), channel_id=1, source_target_pairs={{0,2},{1,3},{2,0},{3,1},{4,6},{5,7},{6,4},{7,5},{8,10},{9,11},{10,... | collective-permute-start | bytes 196616 | tf_op jit(solution)/shard_map/ppermute | solution.py:50
  37.3 8.6 %copy-start.2 = (bf16[1024,512]{1,0:T(8,128)(2,1)S(1)}, bf16[1024,512]{1,0:T(8,128)(2,1)}, u32[]{:S(2)}) copy-start(bf16[1024,512]{1,0:T(8,128)(2,1)} %param.7) | copy-start | bytes 3145732
  41.5 4.3 %collective-permute-start.4 = (f32[128,128]{0,1:T(8,128)S(1)}, f32[128,128]{0,1:T(8,128)S(1)}, u32[]{:S(2)}, u32[]{:S(2)}) collective-permute-start(f32[128,128]{0,1:T(8,128)S(1)} %add.88), channel_id=1, source_target_pairs={{0,4},{1,5},{2,6},{3,7},{4,0},{5,1},{6,2},{7,3},{8,12},{9,13},{10,... | collective-permute-start | bytes 196616 | tf_op jit(solution)/shard_map/ppermute | solution.py:50
  45.8 5.4 %collective-permute-start.5 = (f32[128,128]{0,1:T(8,128)S(1)}, f32[128,128]{0,1:T(8,128)S(1)}, u32[]{:S(2)}, u32[]{:S(2)}) collective-permute-start(f32[128,128]{0,1:T(8,128)S(1)} %add.89), channel_id=1, source_target_pairs={{0,8},{1,9},{2,10},{3,11},{4,12},{5,13},{6,14},{7,15},{8,0},{9,1},... | collective-permute-start | bytes 196616 | tf_op jit(solution)/shard_map/ppermute | solution.py:50
